TPU v7x, 512 devices: a whole 4x8x8 slice. The times are simulated.
512 devices in a mesh: seq: 32 (over x, z), ep: 16 (over y, core).
Axes of the slice: x: 4, y: 8, z: 8, core: 2. Of those that a mesh axis runs over, the one named last changes fastest.
Arguments:
- queries: bfloat16 [16, 4096, 2048], P('ep', 'seq'), may hold values from -6 to 6
- key_rows: bfloat16 [16, 4096, 2048], P('ep', 'seq'), may hold values from -6 to 6
- value_rows: bfloat16 [16, 4096, 2048], P('ep', 'seq'), may hold values from -6 to 6
- residual: bfloat16 [16, 4096, 2048], P('ep', 'seq'), may hold values from -6 to 6
- state_start: float32 [16, 16, 128, 128], P('ep'), may hold values from -192 to 192
- head_gain: float32 [2048], replicated, may hold values from 0.25 to 1.75
- ffn_gain: float32 [2048], replicated, may hold values from 0.25 to 1.75
- routes: int32 [16, 4096, 6], P('ep', 'seq'), may hold values from 0 to 15, all different within a row; in each aligned block of 128 rows (0 to 127, 128 to 255, ..., all dimensions but the last counted through in order) at most 50 rows name the same one
- route_gates: float32 [16, 4096, 6], P('ep', 'seq'), may hold values from 0.1 to 1
- gate_weight: bfloat16 [16, 2048, 704], P('ep', 'seq'), may hold values from -0.125 to 0.125
- up_weight: bfloat16 [16, 2048, 704], P('ep', 'seq'), may hold values from -0.125 to 0.125
- down_weight: bfloat16 [16, 704, 2048], P('ep', None, 'seq'), may hold values from -0.21875 to 0.21875
Outputs:
- layer_out: bfloat16 [16, 4096, 2048], P('ep', 'seq')
Inputs may be any that keep to these rules, and one draw needn't show every extreme that they name: `routes`: each position names 6 different experts. Among the positions of one device (aligned blocks of 128 positions) no expert is named more than 50 times, a bound that some block reaches.
All inputs are finite; a program needn't handle non-finite values.
Results may differ from a plain program's by a relative error of at most 0.015.
Values may be sent and summed in bfloat16 or wider, within the bound.
A program may use at most 128 MiB of HBM per device.

v0:
```python
import jax
import jax.numpy as jnp
from jax import lax
from jax.sharding import PartitionSpec as P

D = 2048
HEADS = 16
HEAD_DIM = 128
EXPERTS = 16
TOP = 6
CAP = 50


def carried_in(array, axis, join, neutral):
    place = lax.axis_index(axis)
    gathered = lax.all_gather(array.astype(jnp.bfloat16), axis)
    state = jnp.zeros_like(array) + jnp.asarray(neutral, array.dtype)

    def one(turn, state):
        return join(state, lax.dynamic_index_in_dim(gathered, turn, 0, False).astype(array.dtype))

    return lax.fori_loop(0, place, one, state)


def route_slots(block_routes):
    chosen = (block_routes[:, None] == jnp.arange(EXPERTS, dtype=jnp.int32)[None, :]).astype(
        jnp.int32
    )
    counts = jnp.cumsum(chosen, axis=0) - 1
    return jnp.sum(chosen * counts, axis=1)


def silu_gate(gate_sum, up_sum):
    return gate_sum / (1.0 + jnp.exp(-gate_sum)) * up_sum


def add_states(earlier, later):
    return earlier + later


def shards(
    queries,
    key_rows,
    value_rows,
    residual,
    state_start,
    head_gain,
    ffn_gain,
    routes,
    route_gates,
    gate_weight,
    up_weight,
    down_weight,
):
    tokens = queries.shape[1]
    query_heads = queries[0].reshape(tokens, HEADS, HEAD_DIM)
    key_heads = key_rows[0].reshape(tokens, HEADS, HEAD_DIM)
    value_heads = value_rows[0].reshape(tokens, HEADS, HEAD_DIM)
    local_state = jnp.einsum(
        "thd,the->hde", key_heads, value_heads, preferred_element_type=jnp.float32
    )
    earlier = carried_in(local_state, "seq", add_states, jnp.zeros_like(local_state))
    state_before = state_start[0] + earlier
    causal = (
        jnp.arange(tokens, dtype=jnp.int32)[:, None] >= jnp.arange(tokens, dtype=jnp.int32)[None, :]
    )
    scores = jnp.einsum("thd,shd->hts", query_heads, key_heads, preferred_element_type=jnp.float32)
    scores = jnp.where(causal[None], scores, 0.0).astype(jnp.bfloat16)
    in_block = jnp.einsum("hts,she->the", scores, value_heads, preferred_element_type=jnp.float32)
    from_state = jnp.einsum(
        "thd,hde->the",
        query_heads.astype(jnp.float32),
        state_before,
        precision=lax.Precision.HIGHEST,
    )
    attended = from_state + in_block
    head_scale = lax.rsqrt(jnp.mean(attended * attended, axis=-1, keepdims=True) + 1e-05)
    head_normed = (attended * head_scale).reshape(tokens, D) * head_gain
    mixed_rows = (residual[0].astype(jnp.float32) + head_normed).astype(jnp.bfloat16)
    mixed_rows = lax.optimization_barrier(mixed_rows)
    mixed_wide = mixed_rows.astype(jnp.float32)
    row_scale = lax.rsqrt(jnp.mean(mixed_wide * mixed_wide, axis=-1, keepdims=True) + 1e-05)
    ffn_in = (mixed_wide * row_scale * ffn_gain).astype(jnp.bfloat16)
    flat_routes = routes[0].reshape(-1)
    slot_rank = route_slots(flat_routes)
    position = flat_routes * CAP + slot_rank
    token_index = jnp.arange(tokens * TOP, dtype=jnp.int32) // TOP
    source = jnp.zeros((EXPERTS * CAP,), jnp.int32).at[position].set(token_index)
    filled = jnp.zeros((EXPERTS * CAP,), jnp.bool_).at[position].set(True)
    outgoing = jnp.where(filled[:, None], ffn_in[source], jnp.zeros((), jnp.bfloat16)).reshape(
        EXPERTS, CAP, D
    )
    arrived = lax.all_to_all(outgoing, "ep", split_axis=0, concat_axis=1, tiled=True)
    whole_gate, whole_up = (
        lax.all_gather(gate_weight, "seq", axis=1, tiled=True),
        lax.all_gather(up_weight, "seq", axis=1, tiled=True),
    )
    gate_sum = jnp.einsum("erd,edh->erh", arrived, whole_gate, preferred_element_type=jnp.float32)
    up_sum = jnp.einsum("erd,edh->erh", arrived, whole_up, preferred_element_type=jnp.float32)
    hidden = silu_gate(gate_sum, up_sum).astype(jnp.bfloat16)
    expert_rows = jnp.einsum(
        "erh,ehd->erd",
        hidden,
        lax.all_gather(down_weight, "seq", axis=2, tiled=True),
        preferred_element_type=jnp.float32,
    ).astype(jnp.bfloat16)
    returned = lax.all_to_all(expert_rows, "ep", split_axis=1, concat_axis=0, tiled=True)
    picked = returned.reshape(EXPERTS * CAP, D)[position].reshape(tokens, TOP, D)
    expert_mix = jnp.sum(route_gates[0][:, :, None] * picked.astype(jnp.float32), axis=1)
    return (mixed_wide + expert_mix).astype(jnp.bfloat16)[None]


def solution(mesh):
    placed = (
        P("ep", "seq", None),
        P("ep", "seq", None),
        P("ep", "seq", None),
        P("ep", "seq", None),
        P("ep", None, None, None),
        P(),
        P(),
        P("ep", "seq", None),
        P("ep", "seq", None),
        P("ep", "seq", None),
        P("ep", "seq", None),
        P("ep", None, "seq"),
    )
    return jax.shard_map(
        shards, mesh=mesh, in_specs=placed, out_specs=P("ep", "seq", None), check_vma=False
    )
```

profile of v0, /device:TPU:1, one launch (start us, length us, event | category | flops | bytes accessed | tf_op | source)
XLA Modules:
  0.0 661.4 jit_solution(5605939818050888803)
XLA Ops:
  6.5 1.4 copy.62
  7.9 1.1 copy.64
  9.1 1.3 convolution_convert_fusion.1
  10.5 0.7 all-gather.8.cloned.1.call-update
  11.2 0.7 all-gather.10.cloned.1.call-update
  12.5 1.7 reduce-window.6
  14.9 3.4 scatter_custom_fusion.1
  18.3 3.4 scatter_custom_fusion
  21.8 140.7 %all-gather.12.cloned.1.call-done = bf16[512,128,128]{2,1,0:T(8,128)(2,1)} async-done(((bf16[16,128,128]{2,1,0:T(8,128)(2,1)}), bf16[512,128,128]{2,1,0:T(8,128)(2,1)}) %all-gather.12.cloned.1.call-update) | async-done | bytes 16777232 | tf_op jit(solution)/shard_map/all_gather | solution.py:16
  162.6 3.2 convolution_bitcast_fusion.1
  165.8 2.1 multiply_reduce_fusion.1
  169.6 4.9 gather_fusion
  174.4 4.7 gather.9
  179.1 4.2 broadcast_select_fusion
  183.3 7.8 %all-to-all-start = ((bf16[16,50,2048]{2,1,0:T(8,128)(2,1)}), bf16[16,50,2048]{2,1,0:T(8,128)(2,1)}, u32[]{:S(2)}, u32[]{:S(2)}) async-start(bf16[16,50,2048]{2,1,0:T(8,128)(2,1)} %broadcast_select_fusion), calls=%async_computation | async-start | bytes 7340032 | tf_op jit(solution)/shard_map/all_to_all | solution.py:93
  191.7 81.8 %all-to-all-done = bf16[16,50,2048]{2,1,0:T(8,128)(2,1)} async-done(((bf16[16,50,2048]{2,1,0:T(8,128)(2,1)}), bf16[16,50,2048]{2,1,0:T(8,128)(2,1)}, u32[]{:S(2)}, u32[]{:S(2)}) %all-to-all-start) | async-done | bytes 3276832 | tf_op jit(solution)/shard_map/all_to_all | solution.py:93
  273.5 3.2 reshape.135
  276.7 7.2 %fusion.1 = f32[800,704]{1,0:T(8,128)} fusion(bf16[800,2048]{1,0:T(8,128)(2,1)S(1)} %reshape.135, bf16[1,2048,704]{2,1,0:T(8,128)(2,1)} %all-gather.8.cloned.1.call-done), kind=kOutput, calls=%fused_computation.10 | convolution fusion | flops 2306867200 | bytes 8413184 | tf_op jit(solution)/shard_map/erd,edh->erh/dot_general | solution.py:99
  284.0 46.2 %all-gather.10.cloned.1.call-done = bf16[1,704,2048]{1,2,0:T(8,128)(2,1)} async-done(((bf16[1,704,64]{1,2,0:T(8,128)(2,1)}), bf16[1,704,2048]{1,2,0:T(8,128)(2,1)}) %all-gather.10.cloned.1.call-update) | async-done | bytes 2883600 | tf_op jit(solution)/shard_map/all_gather | solution.py:104
  330.2 85.3 %all-gather.6.cloned.1.call-done = bf16[1,2048,704]{2,1,0:T(8,128)(2,1)} async-done(((bf16[1,64,704]{2,1,0:T(8,128)(2,1)}), bf16[1,2048,704]{2,1,0:T(8,128)(2,1)}) %all-gather.6.cloned.1.call-update) | async-done | bytes 2883600 | tf_op jit(solution)/shard_map/all_gather | solution.py:95
  415.5 10.5 %fusion.5 = bf16[1,800,2048]{2,1,0:T(8,128)(2,1)S(1)} fusion(bf16[1,704,2048]{1,2,0:T(8,128)(2,1)} %all-gather.10.cloned.1.call-done, f32[800,704]{1,0:T(8,128)} %fusion.1, bf16[800,2048]{1,0:T(8,128)(2,1)} %copy-done.2, bf16[1,2048,704]{2,1,0:T(8,128)(2,1)} %all-gather.6.cloned.1.call-done), kind=kOutput, calls=%fused_computation.14 | convolution fusion | flops 4618188800 | bytes 14573568 | tf_op jit(solution)/shard_map/erh,ehd->erd/dot_general | solution.py:101
  426.0 36.5 %copy.84 = bf16[1,800,2048]{2,0,1:T(2,128)(2,1)} copy(bf16[1,800,2048]{2,1,0:T(8,128)(2,1)S(1)} %fusion.5) | data formatting | bytes 6553600 | tf_op jit(solution)/shard_map/convert_element_type | solution.py:106
  463.1 70.0 %reduce.4 = bf16[800,2048]{1,0:T(8,128)(2,1)S(1)} reduce(bf16[800,1,2048]{2,1,0:T(2,128)(2,1)} %bitcast.74, bf16[]{:T(256)} %broadcast.122), dimensions={1}, to_apply=%bitcast.69.reduce_sub_computation | reduce | bytes 6553602
  533.1 5.1 reshape.183
  538.2 11.6 %all-to-all-start.1 = ((bf16[16,2,51200]{2,1,0:T(2,128)(2,1)}), bf16[16,2,51200]{2,1,0:T(2,128)(2,1)S(1)}, u32[]{:S(2)}, u32[]{:S(2)}) async-start(bf16[16,2,51200]{2,1,0:T(2,128)(2,1)} %reshape.183), calls=%async_computation.1 | async-start | bytes 6553600 | tf_op jit(solution)/shard_map/all_to_all | solution.py:107
  550.0 73.7 %all-to-all-done.1 = bf16[16,2,51200]{2,1,0:T(2,128)(2,1)S(1)} async-done(((bf16[16,2,51200]{2,1,0:T(2,128)(2,1)}), bf16[16,2,51200]{2,1,0:T(2,128)(2,1)S(1)}, u32[]{:S(2)}, u32[]{:S(2)}) %all-to-all-start.1) | async-done | bytes 3276832 | tf_op jit(solution)/shard_map/all_to_all | solution.py:107
  623.7 7.8 %reshape.184 = bf16[800,1,2048]{2,1,0:T(2,128)(2,1)} reshape(bf16[16,2,51200]{2,1,0:T(2,128)(2,1)S(1)} %all-to-all-done.1) | data formatting | bytes 6553600
  631.4 4.9 copy.83
  636.4 4.3 gather_fusion.1
  640.7 6.6 reshape.142
  647.3 6.7 %multiply_reduce_fusion = f32[128,2048]{1,0:T(8,128)S(1)} fusion(f32[128,6,2048]{2,1,0:T(8,128)} %reshape.142, f32[128,6]{1,0:T(8,128)S(1)} %bitcast.86), kind=kLoop, calls=%fused_computation.5 | loop fusion | flops 2883584 | bytes 7343104 | tf_op jit(solution)/shard_map/reduce_sum | solution.py:109
  653.9 0.9 fusion.19
  (55 shorter events, 4.3 us)
Async XLA Ops:
  6.5 5.4 copy-start.5
  6.5 5.8 copy-start.3
  6.5 155.9 %all-gather.12.cloned.1.call-start = ((), (), s32[]{:S(2)}) async-start(), calls=%async_computation.5 | async-start | bytes 17301504 | tf_op jit(solution)/shard_map/all_gather | solution.py:16
  10.4 266.3 %all-gather.8.cloned.1.call-start = ((), (), s32[]{:S(2)}) async-start(), calls=%async_computation.3 | async-start | bytes 3244032 | tf_op jit(solution)/shard_map/all_gather | solution.py:96
  11.2 319.1 %all-gather.10.cloned.1.call-start = ((), (), s32[]{:S(2)}) async-start(), calls=%async_computation.4 | async-start | bytes 3244032 | tf_op jit(solution)/shard_map/all_gather | solution.py:104
  165.8 2.6 copy-start.4
  165.8 2.6 copy-start.6
  168.0 1.4 copy-start.7
  168.6 0.8 copy-start
  183.3 90.2 %all-to-all-start = ((bf16[16,50,2048]{2,1,0:T(8,128)(2,1)}), bf16[16,50,2048]{2,1,0:T(8,128)(2,1)}, u32[]{:S(2)}, u32[]{:S(2)}) async-start(bf16[16,50,2048]{2,1,0:T(8,128)(2,1)} %broadcast_select_fusion), calls=%async_computation | async-start | bytes 7340032 | tf_op jit(solution)/shard_map/all_to_all | solution.py:93
  191.1 224.4 %all-gather.6.cloned.1.call-start = ((), (), s32[]{:S(2)}) async-start(), calls=%async_computation.2 | async-start | bytes 3244032 | tf_op jit(solution)/shard_map/all_gather | solution.py:95
  276.7 7.3 %copy-start.2 = (bf16[800,2048]{1,0:T(8,128)(2,1)}, bf16[800,2048]{1,0:T(8,128)(2,1)S(1)}, u32[]{:S(2)}) copy-start(bf16[800,2048]{1,0:T(8,128)(2,1)S(1)} %reshape.135) | copy-start | bytes 9830404
  538.2 11.7 %copy-start.8 = (f32[1,128,6]{1,0,2:T(1,128)S(1)}, f32[1,128,6]{1,0,2:T(1,128)}, u32[]{:S(2)}) copy-start(f32[1,128,6]{1,0,2:T(1,128)} %param.22) | copy-start | bytes 9220
  538.2 85.5 %all-to-all-start.1 = ((bf16[16,2,51200]{2,1,0:T(2,128)(2,1)}), bf16[16,2,51200]{2,1,0:T(2,128)(2,1)S(1)}, u32[]{:S(2)}, u32[]{:S(2)}) async-start(bf16[16,2,51200]{2,1,0:T(2,128)(2,1)} %reshape.183), calls=%async_computation.1 | async-start | bytes 6553600 | tf_op jit(solution)/shard_map/all_to_all | solution.py:107
  647.2 6.7 %copy-start.1 = (bf16[128,2048]{1,0:T(8,128)(2,1)S(1)}, bf16[128,2048]{1,0:T(8,128)(2,1)}, u32[]{:S(2)}) copy-start(bf16[128,2048]{1,0:T(8,128)(2,1)} %copy-done) | copy-start | bytes 1572868
Sparse Core Ops, SparseCore 0:
  10.5 151.8 all-gather.11
  165.6 79.5 all-gather.7
  248.4 81.7 all-gather.9
  333.2 82.2 all-gather.5
where the time goes:
time: 664 us; the launch traced here: 661 us
  waiting for transfers between devices  429 us (65%)
  local copies, waits for them, and re-layouts  90 us (14%)
  other arithmetic  84.3 us (13%)
  matrix products  24.4 us (4%)
  starting transfers between devices  19.7 us (3%)
  between operations  13.4 us (2%)
    all_gather x1, waiting for transfers between devices, carried_in(): gathered = lax.all_gather(array.astype(jnp.bfloat16), axis)  141 us
    all_gather x1, waiting for transfers between devices, shards(): lax.all_gather(gate_weight, 'seq', axis=1, tiled=True)  85.3 us
    all_to_all x1, waiting for transfers between devices, shards(): lax.all_to_all(outgoing, 'ep', split_axis=0, concat_axis=1, tiled=True)  81.8 us
    all_to_all x1, waiting for transfers between devices, shards(): lax.all_to_all(expert_rows, 'ep', split_axis=1, concat_axis=0, tiled=True)  73.7 us
    unnamed x1, other arithmetic  70 us
    all_gather x1, waiting for transfers between devices, shards(): lax.all_gather(down_weight, 'seq', axis=2, tiled=True)  46.2 us
    convert_element_type x1, local copies, waits for them, and re-layouts, shards(): expert_rows = jnp.einsum('erh,ehd->erd', hidden, lax.all_gather(down_weig...  36.5 us
    unnamed x25, local copies, waits for them, and re-layouts  20.3 us
  transfers between devices with their start and end apart: 6, of which 5 were waited for; matrix products, arithmetic and copies ran while one was open for 6% of the time, Pallas kernels for 0%

commit v1 on v0

v1 whole, which is shorter than its diff:
```python
import functools

import jax
import jax.numpy as jnp
from jax import lax
from jax.experimental import pallas as pl
from jax.experimental.pallas import tpu as pltpu
from jax.sharding import PartitionSpec as P

D = 2048
HALF = 1024
HEADS = 16
HD = 128
HID = 704
EXPERTS = 16
TOP = 6
T = 128
NX, NZ, NY = 4, 8, 8
MESH = pl.DeviceIdType.MESH
F32 = jnp.float32
BF16 = jnp.bfloat16
HIGH = lax.Precision.HIGHEST
TN = (((0,), (0,)), ((), ()))
NT = (((1,), (1,)), ((), ()))
NN = (((1,), (0,)), ((), ()))


def dot(a, b, dims=NN, precision=None):
    return lax.dot_general(a, b, dims, precision=precision, preferred_element_type=F32)


def place():
    seq, ep = lax.axis_index("seq"), lax.axis_index("ep")
    return seq // NZ, lax.rem(seq, NZ), ep // 2, lax.rem(ep, 2)


def ring(at, step, size):
    return lax.rem(at + step + size, size)


def remote(src, dst, send, recv, device):
    return pltpu.make_async_remote_copy(
        src_ref=src, dst_ref=dst, send_sem=send, recv_sem=recv, device_id=device, device_id_type=MESH
    )


def greet(devices):
    barrier = pltpu.get_barrier_semaphore()
    for device in devices:
        pl.semaphore_signal(barrier, inc=1, device_id=device, device_id_type=MESH)
    pl.semaphore_wait(barrier, len(devices))


def cols(h):
    return pl.ds(pl.multiple_of(h * HD, HD), HD)


class YGather:
    def __init__(self, at, units, near, sib_send, sib_recv, send, recv):
        self.x, self.z, self.y, self.c = at
        self.seq = self.x * NZ + self.z
        self.units, self.sends, self.recvs = units, send, recv
        self.sib_send, self.sib_recv = sib_send, sib_recv
        self.pending = []
        del near

    def hop(self, way, w, k):
        block = ring(self.y, -(1 - 2 * way) * (k - 1), NY)
        ref = self.units[w].at[block, self.c]
        to = (self.seq, ring(self.y, 1 - 2 * way, NY) * 2 + self.c)
        n = (way * len(self.units) + w) * 4 + k - 1
        return remote(ref, ref, self.sends.at[n], self.recvs.at[n], to)

    def landed(self, way, w, k):
        block = ring(self.y, -(1 - 2 * way) * k, NY)
        ref = self.units[w].at[block, self.c]
        n = (way * len(self.units) + w) * 4 + k - 1
        return remote(ref, ref, self.sends.at[n], self.recvs.at[n], (self.seq, self.y * 2 + 1 - self.c))

    def across(self, way, w, k, core):
        block = ring(self.y, -(1 - 2 * way) * k, NY)
        ref = self.units[w].at[block, core]
        n = (way * len(self.units) + w) * 5 + k
        return remote(ref, ref, self.sib_send.at[n], self.sib_recv.at[n], (self.seq, self.y * 2 + 1 - self.c))

    def last(self, way, w):
        return way == w % 2

    def start(self, w):
        for way in (0, 1):
            self.hop(way, w, 1).start()
            self.pending.append((way, w, 1))
        self.across(0, w, 0, self.c).start()
        self.crossed = getattr(self, "crossed", []) + [(0, w, 0)]

    def step(self, w, k):
        for way in (0, 1):
            if k == 4 and not self.last(way, w):
                continue
            self.landed(way, w, k).wait_recv()
            if k < 3 or (k == 3 and self.last(way, w)):
                self.hop(way, w, k + 1).start()
                self.pending.append((way, w, k + 1))
            self.across(way, w, k, self.c).start()
            self.crossed.append((way, w, k))

    def finish(self):
        for way, w, k in self.crossed:
            self.across(way, w, k, 1 - self.c).wait_recv()
        for way, w, k in self.pending:
            self.hop(way, w, k).wait_send()
        for way, w, k in self.crossed:
            self.across(way, w, k, self.c).wait_send()


def attend_kernel(
    q, k, v, res, s0, hg, fg, gt,
    rows, gates, mixed,
    mine, parts, back, totals, prior, base,
    z1s, z1r, xs, xr, z2s, z2r, ysend, yrecv, ssend, srecv,
):
    at = x, z, y, c = place()
    seq, ep = x * NZ + z, y * 2 + c
    per = HEADS // NZ
    greet(
        [(x * NZ + ring(z, o, NZ), ep) for o in range(1, NZ)]
        + [(ring(x, o, NX) * NZ + z, ep) for o in range(1, NX)]
        + [(seq, ring(y, o, NY) * 2 + c) for o in (1, -1)]
        + [(seq, y * 2 + 1 - c)]
    )
    gather = YGather(at, [rows.at[:, :, 0], rows.at[:, :, 1], gates], None, ssend, srecv, ysend, yrecv)
    gates[y, c] = gt[...]
    gather.start(2)

    for o in list(range(1, NZ)) + [0]:
        owner = ring(z, o, NZ)
        for i in range(per):
            at_cols = cols(owner * per + i)
            state = dot(k[:, at_cols], v[:, at_cols], TN).astype(BF16)
            if o:
                mine[o, i] = state
            else:
                parts[z, i] = state
        if o:
            remote(mine.at[o], parts.at[z], z1s.at[o], z1r.at[o], (x * NZ + owner, ep)).start()

    causal = lax.broadcasted_iota(jnp.int32, (T, T), 0) >= lax.broadcasted_iota(jnp.int32, (T, T), 1)

    @pl.loop(0, HEADS)
    def _(h):
        at_cols = cols(h)
        qh, kh = q[:, at_cols], k[:, at_cols]
        scores = jnp.where(causal, dot(qh, kh, NT), 0.0).astype(BF16)
        base[:, at_cols] = dot(scores, v[:, at_cols]) + dot(qh.astype(F32), s0[h], precision=HIGH)

    gather.step(2, 1)
    for o in range(1, NZ):
        frm = ring(z, -o, NZ)
        remote(mine.at[o], parts.at[frm], z1s.at[o], z1r.at[o], (x * NZ + frm, ep)).wait_recv()
    total = jnp.zeros((per, HD, HD), F32)
    for o in range(NZ):
        total = total + parts[o].astype(F32)
    totals[x] = total.astype(BF16)
    for o in range(1, NX):
        remote(totals.at[x], totals.at[x], xs.at[o], xr.at[o], (ring(x, o, NX) * NZ + z, ep)).start()
    gather.step(2, 2)
    for o in range(1, NX):
        frm = ring(x, -o, NX)
        remote(totals.at[frm], totals.at[frm], xs.at[o], xr.at[o], (frm * NZ + z, ep)).wait_recv()
    state = jnp.zeros((per, HD, HD), F32)
    for o in range(NX - 1):
        state = state + jnp.where(o < x, totals[o].astype(F32), 0.0)
    for o in range(NZ):
        back[o] = state.astype(BF16)
        state = state + parts[o].astype(F32)
    for o in range(1, NZ):
        to = ring(z, o, NZ)
        remote(back.at[to], prior.at[z], z2s.at[o], z2r.at[o], (x * NZ + to, ep)).start()
    prior[z] = back[z]
    gather.step(2, 3)

    squares = jnp.zeros((T, 1), F32)
    for o in range(NZ):
        owner = ring(z, -o, NZ)
        if o:
            remote(back.at[owner], prior.at[owner], z2s.at[o], z2r.at[o], (x * NZ + owner, ep)).wait_recv()
        for i in range(per):
            at_cols = cols(owner * per + i)
            attended = base[:, at_cols] + dot(q[:, at_cols], prior[owner, i])
            scale = lax.rsqrt(jnp.mean(attended * attended, axis=-1, keepdims=True) + 1e-05)
            normed = attended * scale * hg[:, at_cols]
            row = (res[:, at_cols].astype(F32) + normed).astype(BF16)
            mixed[:, at_cols] = row
            wide = row.astype(F32)
            squares = squares + jnp.sum(wide * wide, axis=-1, keepdims=True)
    row_scale = lax.rsqrt(squares / D + 1e-05)
    for w in (0, 1):
        half = slice(w * HALF, (w + 1) * HALF)
        rows[y, c, w] = (mixed[:, half].astype(F32) * row_scale * fg[:, half]).astype(BF16)
        gather.start(w)
    gather.step(2, 4)
    for k_ in (1, 2, 3, 4):
        for w in (0, 1):
            gather.step(w, k_)
    gather.finish()
    for o in range(1, NZ):
        to = ring(z, o, NZ)
        remote(mine.at[o], parts.at[z], z1s.at[o], z1r.at[o], (x * NZ + to, ep)).wait_send()
        remote(back.at[to], prior.at[z], z2s.at[o], z2r.at[o], (x * NZ + to, ep)).wait_send()
    for o in range(1, NX):
        remote(totals.at[x], totals.at[x], xs.at[o], xr.at[o], (ring(x, o, NX) * NZ + z, ep)).wait_send()


ORDER = (4, 3, -3, 2, -2, 1, -1, 0)


def expert_kernel(
    rows, gates, mixed, gu, dt,
    out,
    hidden, own, sibout, sibin, ringout, ringin, finout, finin,
    ssend, srecv, rsend, rrecv, fsend, frecv,
):
    x, z, y, c = place()
    seq, ep = x * NZ + z, y * 2 + c
    sibling = (seq, y * 2 + 1 - c)
    greet([(seq, ring(y, o, NY) * 2 + c) for o in (1, -1)] + [sibling])
    pick = (lax.broadcasted_iota(jnp.int32, (EXPERTS, HD), 0) == ep).astype(F32)
    low = lax.broadcasted_iota(jnp.int32, (2 * T, HD), 1) < HID % HD

    def silu(gate_sum, up_sum):
        return gate_sum / (1.0 + jnp.exp(-gate_sum)) * up_sum

    def hop(way, j, t):
        n = (way * 4 + j) * 2 + t
        to = (seq, ring(y, 1 - 2 * way, NY) * 2 + c)
        return remote(ringout.at[way, j, t], ringin.at[way, j, t], rsend.at[n], rrecv.at[n], to)

    def cross(n):
        return remote(sibout.at[n], sibin.at[n], ssend.at[n], srecv.at[n], sibling)

    started = []
    for n, off in enumerate(ORDER):
        block = ring(y, off, NY)
        left = rows[block, :, 0].reshape(2 * T, HALF)
        right = rows[block, :, 1].reshape(2 * T, HALF)

        @pl.loop(0, 5)
        def _(i):
            tile = pl.ds(pl.multiple_of(i * 256, 256), 256)
            both = dot(left, gu[:HALF, tile]) + dot(right, gu[HALF:, tile])
            hidden[:, cols(i)] = silu(both[:, :HD], both[:, HD:]).astype(BF16)

        both = dot(left, gu[:HALF, 1280:]) + dot(right, gu[HALF:, 1280:])
        turned = pltpu.roll(both, HD // 2, 1)
        hidden[:, 640:] = jnp.where(low, silu(both, turned), 0.0).astype(BF16)
        gate = jnp.concatenate([dot(gates[block, t], pick, TN, HIGH) for t in (0, 1)], axis=0)
        gate = jnp.concatenate([gate, gate], axis=1)

        @pl.loop(0, 4)
        def _(i):
            tile = pl.ds(pl.multiple_of(i * 256, 256), 256)
            part = dot(hidden[...], dt[1 - c, tile, :], NT) * gate
            sibout[n, :, :, tile] = part.astype(BF16).reshape(2, T, 256)

        cross(n).start()

        @pl.loop(0, 4)
        def _(i):
            tile = pl.ds(pl.multiple_of(i * 256, 256), 256)
            own[:, :, tile] = (dot(hidden[...], dt[c, tile, :], NT) * gate).reshape(2, T, 256)

        cross(n).wait_recv()
        way = 0 if off >= 0 else 1
        for t in (0, 1):
            total = own[t] + sibin[n, t].astype(F32)
            if off == 4:
                ringout[t, 3, t] = total.astype(BF16)
                hop(t, 3, t).start()
                started.append((t, 3, t))
                continue
            j = abs(off)
            for came in (0, 1) if off == 0 else (way,):
                if j == 3 and came != t:
                    continue
                hop(came, j, t).wait_recv()
                total = total + ringin[came, j, t].astype(F32)
            if off:
                ringout[way, j - 1, t] = total.astype(BF16)
                hop(way, j - 1, t).start()
                started.append((way, j - 1, t))
            else:
                own[t] = total

    finout[...] = own[1 - c].astype(BF16)
    final = remote(finout, finin, fsend.at[0], frecv.at[0], sibling)
    final.start()
    mine = pl.ds(pl.multiple_of(c * HALF, HALF), HALF)
    other = pl.ds(pl.multiple_of((1 - c) * HALF, HALF), HALF)
    out[:, mine] = (mixed[:, mine].astype(F32) + own[c]).astype(BF16)
    final.wait()
    out[:, other] = (mixed[:, other].astype(F32) + finin[...].astype(F32)).astype(BF16)
    for way, j, t in started:
        hop(way, j, t).wait_send()
    for n in range(8):
        cross(n).wait_send()


VMEM = pl.BlockSpec(memory_space=pltpu.VMEM)
DMA = pltpu.SemaphoreType.DMA


def shards(q, k, v, res, s0, hg, fg, routes, route_gates, gate_w, up_w, down_w):
    experts = jnp.arange(EXPERTS, dtype=jnp.int32)[:, None]
    chosen, weight = routes[0].T, route_gates[0].T
    gt = jnp.zeros((EXPERTS, T), F32)
    for i in range(TOP):
        gt = gt + jnp.where(chosen[i][None] == experts, weight[i][None], 0.0)
    pieces = []
    for i in range(0, HID, HD):
        pieces += [gate_w[0][:, i : i + HD], up_w[0][:, i : i + HD]]
    gu = lax.all_gather(jnp.concatenate(pieces, axis=1), "seq", axis=0, tiled=True)
    dt = jnp.pad(down_w[0].T, ((0, 0), (0, 768 - HID)))
    dt = lax.all_gather(dt, "seq", axis=0, tiled=True)

    rows, gates, mixed = pl.pallas_call(
        attend_kernel,
        out_shape=(
            jax.ShapeDtypeStruct((NY, 2, 2, T, HALF), BF16),
            jax.ShapeDtypeStruct((NY, 2, EXPERTS, T), F32),
            jax.ShapeDtypeStruct((T, D), BF16),
        ),
        in_specs=[VMEM] * 8,
        out_specs=(VMEM,) * 3,
        scratch_shapes=[
            pltpu.VMEM((NZ, 2, HD, HD), BF16),
            pltpu.VMEM((NZ, 2, HD, HD), BF16),
            pltpu.VMEM((NZ, 2, HD, HD), BF16),
            pltpu.VMEM((NX, 2, HD, HD), BF16),
            pltpu.VMEM((NZ, 2, HD, HD), BF16),
            pltpu.VMEM((T, D), F32),
            DMA((NZ,)), DMA((NZ,)), DMA((NX,)), DMA((NX,)), DMA((NZ,)), DMA((NZ,)),
            DMA((24,)), DMA((24,)), DMA((30,)), DMA((30,)),
        ],
        compiler_params=pltpu.CompilerParams(
            collective_id=0, has_side_effects=True, vmem_limit_bytes=40 * 2**20
        ),
        cost_estimate=pl.CostEstimate(flops=500_000_000, bytes_accessed=300_000_000, transcendentals=0),
        name="attend",
    )(q[0], k[0], v[0], res[0], s0[0], hg[None], fg[None], gt)

    out = pl.pallas_call(
        expert_kernel,
        out_shape=jax.ShapeDtypeStruct((T, D), BF16),
        in_specs=[VMEM] * 5,
        out_specs=VMEM,
        scratch_shapes=[
            pltpu.VMEM((2 * T, 768), BF16),
            pltpu.VMEM((2, T, HALF), F32),
            pltpu.VMEM((8, 2, T, HALF), BF16),
            pltpu.VMEM((8, 2, T, HALF), BF16),
            pltpu.VMEM((2, 4, 2, T, HALF), BF16),
            pltpu.VMEM((2, 4, 2, T, HALF), BF16),
            pltpu.VMEM((T, HALF), BF16),
            pltpu.VMEM((T, HALF), BF16),
            DMA((8,)), DMA((8,)), DMA((16,)), DMA((16,)), DMA((1,)), DMA((1,)),
        ],
        compiler_params=pltpu.CompilerParams(
            collective_id=1, has_side_effects=True, vmem_limit_bytes=56 * 2**20
        ),
        name="experts",
    )(rows, gates, mixed, gu, dt.reshape(2, HALF, 768))
    return out[None]


def solution(mesh):
    placed = (
        P("ep", "seq", None),
        P("ep", "seq", None),
        P("ep", "seq", None),
        P("ep", "seq", None),
        P("ep", None, None, None),
        P(),
        P(),
        P("ep", "seq", None),
        P("ep", "seq", None),
        P("ep", "seq", None),
        P("ep", "seq", None),
        P("ep", None, "seq"),
    )
    return jax.shard_map(
        shards, mesh=mesh, in_specs=placed, out_specs=P("ep", "seq", None), check_vma=False
    )
```

time: 664 us -> 283 us (0.43)
  waiting for transfers between devices: 429 us -> 81.5 us
  Pallas kernels: 0 us -> 168 us
  other arithmetic: 84.3 us -> 0.01 us
  local copies, waits for them, and re-layouts: 90 us -> 19.4 us
  matrix products: 24.4 us -> 0 us
  starting transfers between devices: 19.7 us -> 0.04 us
    all_gather x4 -> x2, waiting for transfers between devices: 272 us -> 81.5 us  [the longest x1 81.5 us: shards(): lax.all_gather(jnp.concatenate(pieces, axis=1), 'seq', axis=0, tiled=True)]
    pallas_call x0 -> x2, Pallas kernels: none -> 168 us  [the longest x1 94.4 us: shards(): pl.pallas_call(attend_kernel, out_shape=(jax.ShapeDtypeStruct((NY, 2, 2,...]
    all_to_all x2 -> x0, waiting for transfers between devices: 155 us -> none  [the longest x1 81.8 us: shards(): lax.all_to_all(outgoing, 'ep', split_axis=0, concat_axis=1, tiled=True)]
    unnamed x1 -> x0, other arithmetic: 70 us -> none
    convert_element_type x2 -> x0, local copies, waits for them, and re-layouts: 43.1 us -> none  [the longest x1 36.5 us: shards(): expert_rows = jnp.einsum('erh,ehd->erd', hidden, lax.all_gather(down_weig...]
    dot_general x5 -> x0, matrix products: 24.4 us -> none  [the longest x1 10.5 us: shards(): jnp.einsum('erh,ehd->erd', hidden, lax.all_gather(down_weight, 'seq', axi...]
    all_to_all x2 -> x0, starting transfers between devices: 19.4 us -> none  [the longest x1 11.6 us: shards(): lax.all_to_all(expert_rows, 'ep', split_axis=1, concat_axis=0, tiled=True)]
    gather x3 -> x0, local copies, waits for them, and re-layouts: 13.9 us -> none  [the longest x2 9.57 us: shards(): ffn_in[source]]
  transfers between devices with their start and end apart: 6 -> 2, of which waited for: 5 -> 1; matrix products, arithmetic and copies ran while one was open for 6% -> 2% of each run, Pallas kernels for 0% -> 33%
where the time goes in v1:
time: 283 us; the launch traced here: 282 us
  Pallas kernels  168 us (59%)
  waiting for transfers between devices  81.5 us (29%)
  local copies, waits for them, and re-layouts  19.4 us (7%)
  between operations  13.5 us (5%)
    pallas_call x1, Pallas kernels, shards(): pl.pallas_call(attend_kernel, out_shape=(jax.ShapeDtypeStruct((NY, 2, 2,...  94.4 us
    all_gather x1, waiting for transfers between devices, shards(): lax.all_gather(jnp.concatenate(pieces, axis=1), 'seq', axis=0, tiled=True)  81.5 us
    pallas_call x1, Pallas kernels, shards(): pl.pallas_call(expert_kernel, out_shape=jax.ShapeDtypeStruct((T, D), BF16...  73.2 us
    unnamed x23, local copies, waits for them, and re-layouts  14.7 us
  transfers between devices with their start and end apart: 2, of which 1 were waited for; matrix products, arithmetic and copies ran while one was open for 2% of the time, Pallas kernels for 33%

profile of v1, /device:TPU:1, one launch (start us, length us, event | category | flops | bytes accessed | tf_op | source)
XLA Modules:
  0.0 282.0 jit_solution(8542968218341791607)
XLA Ops:
  6.5 0.0 all-gather.5.cloned.1.call-start
  6.5 1.6 pad.4
  8.1 0.0 all-gather.5.cloned.1.call-update
  8.1 0.0 all-gather.3.cloned.1.call-start
  8.2 0.7 slice.106
  8.9 0.7 slice.107
  9.6 0.9 fusion
  10.5 0.8 concatenate.3
  11.3 0.0 all-gather.3.cloned.1.call-update
  11.3 0.7 copy.18
  12.0 0.7 copy.17
  12.7 0.0 copy-start.1
  12.7 1.2 copy-done.1
  13.9 0.0 copy-start.3
  13.9 1.0 copy-done.3
  15.0 0.0 copy-start.4
  15.0 1.0 copy-done.4
  16.0 0.0 copy-start.5
  16.0 1.0 copy-done.5
  17.0 0.0 copy-start.6
  17.0 1.0 copy-done.6
  18.1 0.0 copy-start.8
  18.1 0.7 copy-done.8
  18.8 0.7 copy-done.9
  19.5 94.4 %attend.1 = (bf16[8,2,2,128,1024]{4,3,2,1,0:T(8,128)(2,1)S(1)}, f32[8,2,16,128]{3,2,1,0:T(8,128)S(1)}, bf16[128,2048]{1,0:T(8,128)(2,1)S(1)}) custom-call(bf16[128,2048]{1,0:T(8,128)(2,1)S(1)} %bitcast.49, bf16[128,2048]{1,0:T(8,128)(2,1)S(1)} %bitcast.50, bf16[128,2048]{1,0:T(8,128)(2,1)S(1)} %bitcast.51, bf16[128,2048]{1,0:T(8,128)(2,1)S(1)} %bitcast.52, ...), custom_call_target="tpu_custom_call" | custom-call | flops 500000000 | bytes 300000000 | tf_op jit(solution)/shard_map/attend/pallas_call | solution.py:325
  113.9 0.0 copy-start
  113.9 3.2 %copy-done = bf16[8,2,2,128,1024]{4,3,2,1,0:T(8,128)(2,1)} copy-done((bf16[8,2,2,128,1024]{4,3,2,1,0:T(8,128)(2,1)}, bf16[8,2,2,128,1024]{4,3,2,1,0:T(8,128)(2,1)S(1)}, u32[]{:S(2)}) %copy-start) | copy-done | bytes 8388632
  117.1 0.8 copy-done.2
  117.9 0.6 copy-done.7
  118.5 81.5 %all-gather.3.cloned.1.call-done.gu = bf16[2048,1408]{1,0:T(8,128)(2,1)} async-done(((bf16[64,1408]{1,0:T(8,128)(2,1)}), bf16[2048,1408]{1,0:T(8,128)(2,1)}) %all-gather.3.cloned.1.call-update) | async-done | bytes 5767184 | tf_op jit(solution)/shard_map/all_gather | solution.py:321
  200.0 73.2 %experts.1 = bf16[128,2048]{1,0:T(8,128)(2,1)} custom-call(bf16[8,2,2,128,1024]{4,3,2,1,0:T(8,128)(2,1)} %copy-done, f32[8,2,16,128]{3,2,1,0:T(8,128)} %copy-done.7, bf16[128,2048]{1,0:T(8,128)(2,1)} %copy-done.2, bf16[2048,1408]{1,0:T(8,128)(2,1)} %all-gather.3.cloned.1.call-done.gu, bf16[2,1024,768]{2,1,0:T(8,128)(2,1)} %bitcast.55), custom_call_target="tpu_custom_call" | custom-call | tf_op jit(solution)/shard_map/experts/pallas_call | solution.py:351
  273.2 1.9 copy.20
  (7 shorter events, 0.0 us)
Async XLA Ops:
  6.5 112.0 %all-gather.5.cloned.1.call-start = ((), (), s32[]{:S(2)}) async-start(), calls=%async_computation.1 | async-start | bytes 3244032 | tf_op jit(solution)/shard_map/all_gather | solution.py:323
  8.1 191.9 %all-gather.3.cloned.1.call-start = ((), (), s32[]{:S(2)}) async-start(), calls=%async_computation | async-start | bytes 5947392 | tf_op jit(solution)/shard_map/all_gather | solution.py:321
  12.7 1.2 copy-start.1
  13.9 1.0 copy-start.3
  15.0 1.0 copy-start.4
  16.0 1.0 copy-start.5
  17.0 1.0 copy-start.6
  18.1 0.7 copy-start.8
  18.8 0.7 copy-start.9
  113.9 3.2 %copy-start = (bf16[8,2,2,128,1024]{4,3,2,1,0:T(8,128)(2,1)}, bf16[8,2,2,128,1024]{4,3,2,1,0:T(8,128)(2,1)S(1)}, u32[]{:S(2)}) copy-start(bf16[8,2,2,128,1024]{4,3,2,1,0:T(8,128)(2,1)S(1)} %get-tuple-element.8.rows) | copy-start | bytes 25165828
  117.1 0.8 copy-start.2
  117.9 0.7 copy-start.7
Sparse Core Ops, SparseCore 0:
  10.5 94.7 all-gather.4
  108.5 91.5 all-gather.2

commit v2 on v1

v2 whole, which is shorter than its diff:
```python
import functools

import jax
import jax.numpy as jnp
from jax import lax
from jax.experimental import pallas as pl
from jax.experimental.pallas import tpu as pltpu
from jax.sharding import PartitionSpec as P

D = 2048
HALF = 1024
HEADS = 16
HD = 128
HID = 704
EXPERTS = 16
TOP = 6
T = 128
NX, NZ, NY = 4, 8, 8
MESH = pl.DeviceIdType.MESH
F32 = jnp.float32
BF16 = jnp.bfloat16
HIGH = lax.Precision.HIGHEST
TN = (((0,), (0,)), ((), ()))
NT = (((1,), (1,)), ((), ()))
NN = (((1,), (0,)), ((), ()))


def dot(a, b, dims=NN, precision=None):
    return lax.dot_general(a, b, dims, precision=precision, preferred_element_type=F32)


def place():
    seq, ep = lax.axis_index("seq"), lax.axis_index("ep")
    return seq // NZ, lax.rem(seq, NZ), ep // 2, lax.rem(ep, 2)


def ring(at, step, size):
    return lax.rem(at + step + size, size)


def remote(src, dst, send, recv, device):
    return pltpu.make_async_remote_copy(
        src_ref=src, dst_ref=dst, send_sem=send, recv_sem=recv, device_id=device, device_id_type=MESH
    )


def greet(devices):
    barrier = pltpu.get_barrier_semaphore()
    for device in devices:
        pl.semaphore_signal(barrier, inc=1, device_id=device, device_id_type=MESH)
    pl.semaphore_wait(barrier, len(devices))


def cols(h):
    return pl.ds(pl.multiple_of(h * HD, HD), HD)


class Ring:
    def __init__(self, at, n, device, units, send, recv):
        self.at, self.n, self.device, self.units = at, n, device, units
        self.send, self.recv, self.started = send, recv, []

    def block(self, way, k):
        return ring(self.at, -(1 - 2 * way) * k, self.n)

    def copy(self, way, w, k, block):
        ref = self.units[w](block)
        i = (way * len(self.units) + w) * (self.n // 2) + k - 1
        to = self.device(ring(self.at, 1 - 2 * way, self.n))
        return remote(ref, ref, self.send.at[i], self.recv.at[i], to)

    def ways(self, w, k):
        return (0, 1) if k < self.n // 2 else (w % 2,)

    def hop(self, way, w, k):
        self.copy(way, w, k, self.block(way, k - 1)).start()
        self.started.append((way, w, k))

    def start(self, w):
        for way in (0, 1):
            self.hop(way, w, 1)

    def step(self, w, k):
        for way in self.ways(w, k):
            self.copy(way, w, k, self.block(way, k)).wait_recv()
            if k < self.n // 2 and way in self.ways(w, k + 1):
                self.hop(way, w, k + 1)

    def sent(self):
        for way, w, k in self.started:
            self.copy(way, w, k, self.block(way, k - 1)).wait_send()


class PairRing(Ring):
    def __init__(self, at, n, device, units, send, recv, core, sibling, cross_send, cross_recv):
        self.mine = [functools.partial(unit, core=core) for unit in units]
        self.other = [functools.partial(unit, core=1 - core) for unit in units]
        super().__init__(at, n, device, self.mine, send, recv)
        self.sibling, self.cross_send, self.cross_recv = sibling, cross_send, cross_recv
        self.crossed = []

    def across(self, way, w, k, units):
        ref = units[w](self.block(way, k))
        i = (way * len(units) + w) * (self.n // 2 + 1) + k
        return remote(ref, ref, self.cross_send.at[i], self.cross_recv.at[i], self.sibling)

    def cross(self, way, w, k):
        self.across(way, w, k, self.mine).start()
        self.crossed.append((way, w, k))

    def start(self, w):
        super().start(w)
        self.cross(0, w, 0)

    def step(self, w, k):
        super().step(w, k)
        for way in self.ways(w, k):
            self.cross(way, w, k)

    def came_across(self):
        for way, w, k in self.crossed:
            self.across(way, w, k, self.other).wait_recv()

    def sent(self):
        super().sent()
        for way, w, k in self.crossed:
            self.across(way, w, k, self.mine).wait_send()


ORDER = (4, 3, -3, 2, -2, 1, -1, 0)
NEAR = (0, 1, -1, 2, -2, 3, -3, 4)


def kernel(
    q_in, k_in, v_in, res_in, s0_in, gu_in, dt_in, hg, fg, gt,
    out,
    q, k, v, res, s0, gu, dt, rows, gates, mixed,
    mine, parts, back, totals, prior, base,
    hidden, own, sibout, sibin, ringout, ringin, finout, finin,
    load, z1s, z1r, xs, xr, z2s, z2r, ys, yr, ycs, ycr, gs, gr, gcs, gcr,
    gzs, gzr, gxs, gxr, dxs, dxr, dzs, dzr, ss, sr, rs, rr, fs, fr,
):
    x, z, y, c = place()
    seq, ep = x * NZ + z, y * 2 + c
    per = HEADS // NZ
    sibling = (seq, y * 2 + 1 - c)
    loads = [
        pltpu.make_async_copy(src, dst, load.at[i])
        for i, (src, dst) in enumerate(
            [(k_in, k), (v_in, v), (gu_in, gu.at[x, z]), (dt_in, dt.at[x, z]), (q_in, q), (s0_in, s0), (res_in, res)]
        )
    ]
    for one in loads:
        one.start()
    greet(
        [(x * NZ + ring(z, o, NZ), ep) for o in range(1, NZ)]
        + [(ring(x, o, NX) * NZ + z, ep) for o in range(1, NX)]
        + [(seq, ring(y, o, NY) * 2 + c) for o in (1, -1)]
        + [sibling]
    )

    def on_x(place):
        return place * NZ + z, ep

    def on_y(place):
        return seq, place * 2 + c

    def on_z(place):
        return x * NZ + place, ep

    tokens = PairRing(
        y, NY, on_y, [lambda b, core, w=w: rows.at[b, core, w] for w in (0, 1)], ys, yr, c, sibling, ycs, ycr
    )
    gate_ring = PairRing(y, NY, on_y, [lambda b, core: gates.at[b, core]], gs, gr, c, sibling, gcs, gcr)
    up_z = Ring(z, NZ, on_z, [lambda b, w=w: gu.at[x, b, pl.ds(w * 32, 32)] for w in (0, 1)], gzs, gzr)
    up_x = Ring(x, NX, on_x, [lambda b, o=o: gu.at[b, ring(z, o, NZ)] for o in NEAR], gxs, gxr)
    down_z = Ring(z, NZ, on_z, [lambda b, w=w: dt.at[pl.ds(w * 2, 2), b] for w in (0, 1)], dzs, dzr)

    def down_x(o, frm):
        ref = dt.at[frm, z]
        return remote(ref, ref, dxs.at[o], dxr.at[o], on_x(ring(x, o, NX)))

    gates[y, c] = gt[...]
    gate_ring.start(0)

    loads[0].wait()
    loads[1].wait()
    for o in list(range(1, NZ)) + [0]:
        owner = ring(z, o, NZ)
        for i in range(per):
            at_cols = cols(owner * per + i)
            state = dot(k[:, at_cols], v[:, at_cols], TN).astype(BF16)
            if o:
                mine[o, i] = state
            else:
                parts[z, i] = state
        if o:
            remote(mine.at[o], parts.at[z], z1s.at[o], z1r.at[o], on_z(owner)).start()
    loads[2].wait()
    for w in (0, 1):
        up_z.start(w)
    up_x.start(0)
    loads[3].wait()
    for o in range(1, NX):
        down_x(o, x).start()

    causal = lax.broadcasted_iota(jnp.int32, (T, T), 0) >= lax.broadcasted_iota(jnp.int32, (T, T), 1)
    loads[4].wait()
    loads[5].wait()

    @pl.loop(0, HEADS)
    def _(h):
        at_cols = cols(h)
        qh, kh = q[:, at_cols], k[:, at_cols]
        scores = jnp.where(causal, dot(qh, kh, NT), 0.0).astype(BF16)
        base[:, at_cols] = dot(scores, v[:, at_cols]) + dot(qh.astype(F32), s0[h], precision=HIGH)

    def up_step(n):
        for w in (0, 1):
            up_z.step(w, n)
        for w, o in enumerate(NEAR):
            if abs(o) == n:
                up_x.start(w)

    gate_ring.step(0, 1)
    for o in range(1, NZ):
        frm = ring(z, -o, NZ)
        remote(mine.at[o], parts.at[frm], z1s.at[o], z1r.at[o], on_z(frm)).wait_recv()
    total = jnp.zeros((per, HD, HD), F32)
    for o in range(NZ):
        total = total + parts[o].astype(F32)
    totals[x] = total.astype(BF16)
    for o in range(1, NX):
        remote(totals.at[x], totals.at[x], xs.at[o], xr.at[o], on_x(ring(x, o, NX))).start()
    up_step(1)
    gate_ring.step(0, 2)
    for o in range(1, NX):
        frm = ring(x, -o, NX)
        remote(totals.at[frm], totals.at[frm], xs.at[o], xr.at[o], on_x(frm)).wait_recv()
    state = jnp.zeros((per, HD, HD), F32)
    for o in range(NX - 1):
        state = state + jnp.where(o < x, totals[o].astype(F32), 0.0)
    for o in range(NZ):
        back[o] = state.astype(BF16)
        state = state + parts[o].astype(F32)
    for o in range(1, NZ):
        to = ring(z, o, NZ)
        remote(back.at[to], prior.at[z], z2s.at[o], z2r.at[o], on_z(to)).start()
    prior[z] = back[z]
    up_step(2)
    gate_ring.step(0, 3)
    up_x.step(0, 1)
    for o in range(1, NX):
        down_x(o, ring(x, -o, NX)).wait_recv()
    loads[6].wait()

    squares = jnp.zeros((T, 1), F32)
    for o in range(NZ):
        owner = ring(z, -o, NZ)
        if o:
            remote(back.at[owner], prior.at[owner], z2s.at[o], z2r.at[o], on_z(owner)).wait_recv()
        for i in range(per):
            at_cols = cols(owner * per + i)
            attended = base[:, at_cols] + dot(q[:, at_cols], prior[owner, i])
            scale = lax.rsqrt(jnp.mean(attended * attended, axis=-1, keepdims=True) + 1e-05)
            normed = attended * scale * hg[:, at_cols]
            row = (res[:, at_cols].astype(F32) + normed).astype(BF16)
            mixed[:, at_cols] = row
            wide = row.astype(F32)
            squares = squares + jnp.sum(wide * wide, axis=-1, keepdims=True)
    row_scale = lax.rsqrt(squares / D + 1e-05)
    for w in (0, 1):
        half = slice(w * HALF, (w + 1) * HALF)
        rows[y, c, w] = (mixed[:, half].astype(F32) * row_scale * fg[:, half]).astype(BF16)
        tokens.start(w)
    up_step(3)
    for w in (0, 1):
        down_z.start(w)
    gate_ring.step(0, 4)
    up_step(4)
    for n in range(1, 5):
        for w in (0, 1):
            tokens.step(w, n)
            if n == 1:
                up_x.step(w + 1, 1)
                down_z.step(w, 1)
            else:
                if 2 * n + w - 1 < len(NEAR):
                    up_x.step(2 * n + w - 1, 1)
                up_x.step(2 * n + w - 4, 2)
                down_z.step(w, n)
    up_x.step(6, 2)
    up_x.step(7, 2)
    gate_ring.came_across()
    tokens.came_across()

    pick = (lax.broadcasted_iota(jnp.int32, (EXPERTS, HD), 0) == ep).astype(F32)
    low = lax.broadcasted_iota(jnp.int32, (2 * T, HD), 1) < HID % HD

    def silu(gate_sum, up_sum):
        return gate_sum / (1.0 + jnp.exp(-gate_sum)) * up_sum

    def hop(way, j, t):
        n = (way * 4 + j) * 2 + t
        to = on_y(ring(y, 1 - 2 * way, NY))
        return remote(ringout.at[way, j, t], ringin.at[way, j, t], rs.at[n], rr.at[n], to)

    def cross(n):
        return remote(sibout.at[n], sibin.at[n], ss.at[n], sr.at[n], sibling)

    def up_tile(left, right, tile):
        top = gu[0:2, :, :, tile].reshape(HALF, -1)
        bottom = gu[2:4, :, :, tile].reshape(HALF, -1)
        return dot(left, top) + dot(right, bottom)

    def down_tile(half, i):
        piece = dt[half * 2 + i // 2, pl.ds(lax.rem(i, 2) * 4, 4)]
        return dot(hidden[...], piece.reshape(256, 768), NT)

    started = []
    for n, off in enumerate(ORDER):
        block = ring(y, off, NY)
        left = rows[block, :, 0].reshape(2 * T, HALF)
        right = rows[block, :, 1].reshape(2 * T, HALF)

        @pl.loop(0, 5)
        def _(i):
            both = up_tile(left, right, pl.ds(pl.multiple_of(i * 256, 256), 256))
            hidden[:, cols(i)] = silu(both[:, :HD], both[:, HD:]).astype(BF16)

        both = up_tile(left, right, pl.ds(1280, HD))
        turned = pltpu.roll(both, HD // 2, 1)
        hidden[:, 640:] = jnp.where(low, silu(both, turned), 0.0).astype(BF16)
        gate = jnp.concatenate([dot(gates[block, t], pick, TN, HIGH) for t in (0, 1)], axis=0)
        gate = jnp.concatenate([gate, gate], axis=1)

        @pl.loop(0, 4)
        def _(i):
            part = down_tile(1 - c, i) * gate
            sibout[n, :, :, pl.ds(pl.multiple_of(i * 256, 256), 256)] = part.astype(BF16).reshape(2, T, 256)

        cross(n).start()

        @pl.loop(0, 4)
        def _(i):
            part = down_tile(c, i) * gate
            own[:, :, pl.ds(pl.multiple_of(i * 256, 256), 256)] = part.reshape(2, T, 256)

        cross(n).wait_recv()
        way = 0 if off >= 0 else 1
        for t in (0, 1):
            total = own[t] + sibin[n, t].astype(F32)
            if off == 4:
                ringout[t, 3, t] = total.astype(BF16)
                hop(t, 3, t).start()
                started.append((t, 3, t))
                continue
            j = abs(off)
            for came in (0, 1) if off == 0 else (way,):
                if j == 3 and came != t:
                    continue
                hop(came, j, t).wait_recv()
                total = total + ringin[came, j, t].astype(F32)
            if off:
                ringout[way, j - 1, t] = total.astype(BF16)
                hop(way, j - 1, t).start()
                started.append((way, j - 1, t))
            else:
                own[t] = total

    finout[...] = own[1 - c].astype(BF16)
    final = remote(finout, finin, fs.at[0], fr.at[0], sibling)
    final.start()
    here = pl.ds(pl.multiple_of(c * HALF, HALF), HALF)
    there = pl.ds(pl.multiple_of((1 - c) * HALF, HALF), HALF)
    out[:, here] = (mixed[:, here].astype(F32) + own[c]).astype(BF16)
    final.wait()
    out[:, there] = (mixed[:, there].astype(F32) + finin[...].astype(F32)).astype(BF16)

    for way, j, t in started:
        hop(way, j, t).wait_send()
    for n in range(8):
        cross(n).wait_send()
    for one in (tokens, gate_ring, up_z, up_x, down_z):
        one.sent()
    for o in range(1, NZ):
        to = ring(z, o, NZ)
        remote(mine.at[o], parts.at[z], z1s.at[o], z1r.at[o], on_z(to)).wait_send()
        remote(back.at[to], prior.at[z], z2s.at[o], z2r.at[o], on_z(to)).wait_send()
    for o in range(1, NX):
        remote(totals.at[x], totals.at[x], xs.at[o], xr.at[o], on_x(ring(x, o, NX))).wait_send()
        down_x(o, x).wait_send()


VMEM = pl.BlockSpec(memory_space=pltpu.VMEM)
ANY = pl.BlockSpec(memory_space=pl.ANY)
DMA = pltpu.SemaphoreType.DMA


def shards(q, k, v, res, s0, hg, fg, routes, route_gates, gate_w, up_w, down_w):
    experts = jnp.arange(EXPERTS, dtype=jnp.int32)[:, None]
    chosen, weight = routes[0].T, route_gates[0].T
    gt = jnp.zeros((EXPERTS, T), F32)
    for i in range(TOP):
        gt = gt + jnp.where(chosen[i][None] == experts, weight[i][None], 0.0)
    pieces = []
    for i in range(0, HID, HD):
        pieces += [gate_w[0][:, i : i + HD], up_w[0][:, i : i + HD]]
    gu = jnp.concatenate(pieces, axis=1)
    dt = jnp.pad(down_w[0].T, ((0, 0), (0, 768 - HID)))
    out = pl.pallas_call(
        kernel,
        out_shape=jax.ShapeDtypeStruct((T, D), BF16),
        in_specs=[ANY] * 7 + [VMEM] * 3,
        out_specs=VMEM,
        scratch_shapes=[
            pltpu.VMEM((T, D), BF16),
            pltpu.VMEM((T, D), BF16),
            pltpu.VMEM((T, D), BF16),
            pltpu.VMEM((T, D), BF16),
            pltpu.VMEM((HEADS, HD, HD), F32),
            pltpu.VMEM((NX, NZ, 64, 2 * HID), BF16),
            pltpu.VMEM((NX, NZ, 64, 768), BF16),
            pltpu.VMEM((NY, 2, 2, T, HALF), BF16),
            pltpu.VMEM((NY, 2, EXPERTS, T), F32),
            pltpu.VMEM((T, D), BF16),
            pltpu.VMEM((NZ, 2, HD, HD), BF16),
            pltpu.VMEM((NZ, 2, HD, HD), BF16),
            pltpu.VMEM((NZ, 2, HD, HD), BF16),
            pltpu.VMEM((NX, 2, HD, HD), BF16),
            pltpu.VMEM((NZ, 2, HD, HD), BF16),
            pltpu.VMEM((T, D), F32),
            pltpu.VMEM((2 * T, 768), BF16),
            pltpu.VMEM((2, T, HALF), F32),
            pltpu.VMEM((8, 2, T, HALF), BF16),
            pltpu.VMEM((8, 2, T, HALF), BF16),
            pltpu.VMEM((2, 4, 2, T, HALF), BF16),
            pltpu.VMEM((2, 4, 2, T, HALF), BF16),
            pltpu.VMEM((T, HALF), BF16),
            pltpu.VMEM((T, HALF), BF16),
            DMA((7,)),
            DMA((NZ,)), DMA((NZ,)), DMA((NX,)), DMA((NX,)), DMA((NZ,)), DMA((NZ,)),
            DMA((16,)), DMA((16,)), DMA((20,)), DMA((20,)),
            DMA((8,)), DMA((8,)), DMA((10,)), DMA((10,)),
            DMA((16,)), DMA((16,)), DMA((32,)), DMA((32,)),
            DMA((NX,)), DMA((NX,)), DMA((16,)), DMA((16,)),
            DMA((8,)), DMA((8,)), DMA((16,)), DMA((16,)), DMA((1,)), DMA((1,)),
        ],
        compiler_params=pltpu.CompilerParams(
            collective_id=0, has_side_effects=True, vmem_limit_bytes=56 * 2**20
        ),
        name="layer",
    )(q[0], k[0], v[0], res[0], s0[0], gu, dt, hg[None], fg[None], gt)
    return out[None]


def solution(mesh):
    placed = (
        P("ep", "seq", None),
        P("ep", "seq", None),
        P("ep", "seq", None),
        P("ep", "seq", None),
        P("ep", None, None, None),
        P(),
        P(),
        P("ep", "seq", None),
        P("ep", "seq", None),
        P("ep", "seq", None),
        P("ep", "seq", None),
        P("ep", None, "seq"),
    )
    return jax.shard_map(
        shards, mesh=mesh, in_specs=placed, out_specs=P("ep", "seq", None), check_vma=False
    )
```

time: 283 us -> 166 us (0.59)
  waiting for transfers between devices: 81.5 us -> 0 us
  between operations: 13.5 us -> 0.03 us
  local copies, waits for them, and re-layouts: 19.4 us -> 6.39 us
  Pallas kernels: 168 us -> 158 us
    all_gather x2 -> x0, waiting for transfers between devices: 81.5 us -> none  [the longest x1 81.5 us: shards(): lax.all_gather(jnp.concatenate(pieces, axis=1), 'seq', axis=0, tiled=True)]
    unnamed x23 -> x7, local copies, waits for them, and re-layouts: 14.7 us -> 3.29 us
    pallas_call x2 -> x1, Pallas kernels: 168 us -> 158 us  [shards(): pl.pallas_call(kernel, out_shape=jax.ShapeDtypeStruct((T, D), BF16), in_s...]
  transfers between devices with their start and end apart: 2 -> 0, of which waited for: 1 -> 0; matrix products, arithmetic and copies ran while one was open for 2% -> 0% of each run, Pallas kernels for 33% -> 0%
where the time goes in v2:
time: 166 us; the launch traced here: 165 us
  Pallas kernels  158 us (95%)
  local copies, waits for them, and re-layouts  6.39 us (4%)
    pallas_call x1, Pallas kernels, shards(): pl.pallas_call(kernel, out_shape=jax.ShapeDtypeStruct((T, D), BF16), in_s...  158 us

profile of v2, /device:TPU:1, one launch (start us, length us, event | category | flops | bytes accessed | tf_op | source)
XLA Modules:
  0.0 165.2 jit_solution(18242797251167363910)
XLA Ops:
  0.0 0.0 copy-start
  0.0 0.7 copy.18
  0.7 0.7 copy.17
  1.4 0.6 select_add_fusion.gt
  2.0 0.7 slice.106
  2.8 0.0 copy-done
  2.8 0.0 copy-start.1
  2.8 1.6 pad.4.dt_in
  4.3 0.0 copy-done.1
  4.4 0.8 concatenate.3.gu_in
  5.1 158.2 %layer.1 = bf16[128,2048]{1,0:T(8,128)(2,1)} custom-call(bf16[128,2048]{1,0:T(8,128)(2,1)} %bitcast.49, bf16[128,2048]{1,0:T(8,128)(2,1)} %bitcast.50, bf16[128,2048]{1,0:T(8,128)(2,1)} %bitcast.51, bf16[128,2048]{1,0:T(8,128)(2,1)} %bitcast.52, f32[16,128,128]{2,1,0:T(8,128)} %bitcast.48, bf16[64,1408]{1,0:T(8,128)(2,1)} %concatenate.3.gu_in, ...), custom_call_target="tpu_custom_call" | custom-call | tf_op jit(solution)/shard_map/layer/pallas_call | solution.py:411
  163.3 1.9 %copy.20 = bf16[1,128,2048]{2,1,0:T(8,128)(2,1)} copy(bf16[1,128,2048]{2,1,0:T(8,128)(2,1)} %bitcast.47) | data formatting | bytes 1048576
  (4 shorter events, 0.0 us)
Async XLA Ops:
  0.0 2.8 %copy-start = (bf16[1,64,704]{2,1,0:T(8,128)(2,1)S(1)}, bf16[1,64,704]{2,1,0:T(8,128)(2,1)}, u32[]{:S(2)}) copy-start(bf16[1,64,704]{2,1,0:T(8,128)(2,1)} %param.22) | copy-start | bytes 270340
  2.8 1.6 copy-start.1

commit v3 on v2

--- a/solution.py
+++ b/solution.py
@@ -44,13 +44,6 @@
     )
 
 
-def greet(devices):
-    barrier = pltpu.get_barrier_semaphore()
-    for device in devices:
-        pl.semaphore_signal(barrier, inc=1, device_id=device, device_id_type=MESH)
-    pl.semaphore_wait(barrier, len(devices))
-
-
 def cols(h):
     return pl.ds(pl.multiple_of(h * HD, HD), HD)
 
@@ -117,9 +110,10 @@
         for way in self.ways(w, k):
             self.cross(way, w, k)
 
-    def came_across(self):
+    def came_across(self, steps):
         for way, w, k in self.crossed:
-            self.across(way, w, k, self.other).wait_recv()
+            if k in steps:
+                self.across(way, w, k, self.other).wait_recv()
 
     def sent(self):
         super().sent()
@@ -127,16 +121,15 @@
             self.across(way, w, k, self.mine).wait_send()
 
 
-ORDER = (4, 3, -3, 2, -2, 1, -1, 0)
 NEAR = (0, 1, -1, 2, -2, 3, -3, 4)
 
 
 def kernel(
-    q_in, k_in, v_in, res_in, s0_in, gu_in, dt_in, hg, fg, gt,
+    q_in, k_in, v_in, res_in, s0_in, gate_in, up_in, down_in, hg, fg, gt,
     out,
     q, k, v, res, s0, gu, dt, rows, gates, mixed,
     mine, parts, back, totals, prior, base,
-    hidden, own, sibout, sibin, ringout, ringin, finout, finin,
+    gate_col, hidden, own, last, sibout, sibin, ringout, ringin, finout, finin,
     load, z1s, z1r, xs, xr, z2s, z2r, ys, yr, ycs, ycr, gs, gr, gcs, gcr,
     gzs, gzr, gxs, gxr, dxs, dxr, dzs, dzr, ss, sr, rs, rr, fs, fr,
 ):
@@ -147,17 +140,28 @@
     loads = [
         pltpu.make_async_copy(src, dst, load.at[i])
         for i, (src, dst) in enumerate(
-            [(k_in, k), (v_in, v), (gu_in, gu.at[x, z]), (dt_in, dt.at[x, z]), (q_in, q), (s0_in, s0), (res_in, res)]
+            [(k_in, k), (v_in, v), (q_in, q), (s0_in, s0), (res_in, res)]
         )
     ]
     for one in loads:
         one.start()
-    greet(
+    near = (
         [(x * NZ + ring(z, o, NZ), ep) for o in range(1, NZ)]
         + [(ring(x, o, NX) * NZ + z, ep) for o in range(1, NX)]
         + [(seq, ring(y, o, NY) * 2 + c) for o in (1, -1)]
         + [sibling]
     )
+    barrier = pltpu.get_barrier_semaphore()
+    for device in near:
+        pl.semaphore_signal(barrier, inc=1, device_id=device, device_id_type=MESH)
+    for i in range(5):
+        here = slice(i * HD, (i + 1) * HD)
+        gu[x, z, :, i * 256 : i * 256 + HD] = gate_in[:, here]
+        gu[x, z, :, i * 256 + HD : (i + 1) * 256] = up_in[:, here]
+    gu[x, z, :, 1280:] = jnp.concatenate([gate_in[:, 640:], up_in[:, 640:]], axis=1)
+    dt[x, z] = jnp.concatenate([down_in[...], jnp.zeros((64, 768 - HID), BF16)], axis=1)
+    gates[y, c] = gt[...]
+    pl.semaphore_wait(barrier, len(near))
 
     def on_x(place):
         return place * NZ + z, ep
@@ -180,7 +184,6 @@
         ref = dt.at[frm, z]
         return remote(ref, ref, dxs.at[o], dxr.at[o], on_x(ring(x, o, NX)))
 
-    gates[y, c] = gt[...]
     gate_ring.start(0)
 
     loads[0].wait()
@@ -196,17 +199,15 @@
                 parts[z, i] = state
         if o:
             remote(mine.at[o], parts.at[z], z1s.at[o], z1r.at[o], on_z(owner)).start()
-    loads[2].wait()
     for w in (0, 1):
         up_z.start(w)
     up_x.start(0)
-    loads[3].wait()
     for o in range(1, NX):
         down_x(o, x).start()
 
     causal = lax.broadcasted_iota(jnp.int32, (T, T), 0) >= lax.broadcasted_iota(jnp.int32, (T, T), 1)
-    loads[4].wait()
-    loads[5].wait()
+    loads[2].wait()
+    loads[3].wait()
 
     @pl.loop(0, HEADS)
     def _(h):
@@ -252,7 +253,7 @@
     up_x.step(0, 1)
     for o in range(1, NX):
         down_x(o, ring(x, -o, NX)).wait_recv()
-    loads[6].wait()
+    loads[4].wait()
 
     squares = jnp.zeros((T, 1), F32)
     for o in range(NZ):
@@ -278,7 +279,7 @@
         down_z.start(w)
     gate_ring.step(0, 4)
     up_step(4)
-    for n in range(1, 5):
+    for n in range(1, 4):
         for w in (0, 1):
             tokens.step(w, n)
             if n == 1:
@@ -289,98 +290,145 @@
                     up_x.step(2 * n + w - 1, 1)
                 up_x.step(2 * n + w - 4, 2)
                 down_z.step(w, n)
-    up_x.step(6, 2)
-    up_x.step(7, 2)
-    gate_ring.came_across()
-    tokens.came_across()
-
+    gate_ring.came_across(range(5))
     pick = (lax.broadcasted_iota(jnp.int32, (EXPERTS, HD), 0) == ep).astype(F32)
-    low = lax.broadcasted_iota(jnp.int32, (2 * T, HD), 1) < HID % HD
+
+    @pl.loop(0, NY)
+    def _(b):
+        for t in (0, 1):
+            gate_col[b, t] = dot(gates[b, t], pick, TN, HIGH)
+
+    low = lax.broadcasted_iota(jnp.int32, (1, HD), 1) < HID % HD
 
     def silu(gate_sum, up_sum):
         return gate_sum / (1.0 + jnp.exp(-gate_sum)) * up_sum
+
+    def stack(parts):
+        return parts[0] if len(parts) == 1 else jnp.concatenate(parts, axis=0)
+
+    def expert_in(offs):
+        blocks = [ring(y, off, NY) for off in offs]
+        left, right = (stack([rows[b, :, u].reshape(2 * T, HALF) for b in blocks]) for u in (0, 1))
+
+        def up_tile(tile):
+            top = gu[0:2, :, :, tile].reshape(HALF, -1)
+            bottom = gu[2:4, :, :, tile].reshape(HALF, -1)
+            return dot(left, top) + dot(right, bottom)
+
+        def keep(i, value):
+            for n, off in enumerate(offs):
+                hidden[off % NY, :, i * HD : (i + 1) * HD] = value[n * 2 * T : (n + 1) * 2 * T].astype(BF16)
+
+        for i in range(5):
+            both = up_tile(slice(i * 256, (i + 1) * 256))
+            keep(i, silu(both[:, :HD], both[:, HD:]))
+        both = up_tile(slice(1280, 1408))
+        keep(5, jnp.where(low, silu(both, pltpu.roll(both, HD // 2, 1)), 0.0))
 
     def hop(way, j, t):
         n = (way * 4 + j) * 2 + t
         to = on_y(ring(y, 1 - 2 * way, NY))
         return remote(ringout.at[way, j, t], ringin.at[way, j, t], rs.at[n], rr.at[n], to)
 
-    def cross(n):
+    def cross(off):
+        n = off % NY
         return remote(sibout.at[n], sibin.at[n], ss.at[n], sr.at[n], sibling)
 
-    def up_tile(left, right, tile):
-        top = gu[0:2, :, :, tile].reshape(HALF, -1)
-        bottom = gu[2:4, :, :, tile].reshape(HALF, -1)
-        return dot(left, top) + dot(right, bottom)
-
-    def down_tile(half, i):
-        piece = dt[half * 2 + i // 2, pl.ds(lax.rem(i, 2) * 4, 4)]
-        return dot(hidden[...], piece.reshape(256, 768), NT)
+    def expert_out(offs, keep):
+        blocks = [ring(y, off, NY) for off in offs]
+        rows_in = stack([hidden[off % NY] for off in offs])
+        gate = stack([gate_col[b].reshape(2 * T, HD) for b in blocks])
+        gate = jnp.concatenate([gate, gate], axis=1)
+
+        def down_tile(half, i):
+            piece = dt[half * 2 + i // 2, (i % 2) * 4 : (i % 2) * 4 + 4]
+            return dot(rows_in, piece.reshape(256, 768), NT) * gate
+
+        for i in range(4):
+            part = down_tile(1 - c, i).astype(BF16)
+            for n, off in enumerate(offs):
+                sibout[off % NY, :, :, i * 256 : (i + 1) * 256] = part[n * 2 * T : (n + 1) * 2 * T].reshape(2, T, 256)
+        for off in offs:
+            cross(off).start()
+        for i in range(4):
+            part = down_tile(c, i)
+            for n in range(len(offs)):
+                keep[n, :, :, i * 256 : (i + 1) * 256] = part[n * 2 * T : (n + 1) * 2 * T].reshape(2, T, 256)
 
     started = []
-    for n, off in enumerate(ORDER):
-        block = ring(y, off, NY)
-        left = rows[block, :, 0].reshape(2 * T, HALF)
-        right = rows[block, :, 1].reshape(2 * T, HALF)
-
-        @pl.loop(0, 5)
-        def _(i):
-            both = up_tile(left, right, pl.ds(pl.multiple_of(i * 256, 256), 256))
-            hidden[:, cols(i)] = silu(both[:, :HD], both[:, HD:]).astype(BF16)
-
-        both = up_tile(left, right, pl.ds(1280, HD))
-        turned = pltpu.roll(both, HD // 2, 1)
-        hidden[:, 640:] = jnp.where(low, silu(both, turned), 0.0).astype(BF16)
-        gate = jnp.concatenate([dot(gates[block, t], pick, TN, HIGH) for t in (0, 1)], axis=0)
-        gate = jnp.concatenate([gate, gate], axis=1)
-
-        @pl.loop(0, 4)
-        def _(i):
-            part = down_tile(1 - c, i) * gate
-            sibout[n, :, :, pl.ds(pl.multiple_of(i * 256, 256), 256)] = part.astype(BF16).reshape(2, T, 256)
-
-        cross(n).start()
-
-        @pl.loop(0, 4)
-        def _(i):
-            part = down_tile(c, i) * gate
-            own[:, :, pl.ds(pl.multiple_of(i * 256, 256), 256)] = part.reshape(2, T, 256)
-
-        cross(n).wait_recv()
-        way = 0 if off >= 0 else 1
-        for t in (0, 1):
-            total = own[t] + sibin[n, t].astype(F32)
-            if off == 4:
-                ringout[t, 3, t] = total.astype(BF16)
-                hop(t, 3, t).start()
-                started.append((t, 3, t))
-                continue
-            j = abs(off)
-            for came in (0, 1) if off == 0 else (way,):
-                if j == 3 and came != t:
-                    continue
-                hop(came, j, t).wait_recv()
-                total = total + ringin[came, j, t].astype(F32)
-            if off:
-                ringout[way, j - 1, t] = total.astype(BF16)
-                hop(way, j - 1, t).start()
-                started.append((way, j - 1, t))
-            else:
-                own[t] = total
-
-    finout[...] = own[1 - c].astype(BF16)
+
+    def send(way, j, t, total):
+        ringout[way, j, t] = total.astype(BF16)
+        hop(way, j, t).start()
+        started.append((way, j, t))
+
+    def pass_on(j, turn):
+        for way in (0, 1):
+            t = turn ^ 1 ^ way
+            total = own[j - 1, way, t] + sibin[(j, NY - j)[way], t].astype(F32)
+            if j < 3 or turn:
+                hop(way, j, t).wait_recv()
+                total = total + ringin[way, j, t].astype(F32)
+            send(way, j - 1, t, total)
+
+    up_x.step(7, 1)
+    for n in (4, 5, 6, 7):
+        up_x.step(n, 2)
+    tokens.came_across((0, 1, 2, 3))
+    expert_in((3, -3))
+    tokens.step(0, 4)
+    tokens.step(1, 4)
+    down_z.step(0, 4)
+    down_z.step(1, 4)
+    expert_out((3, -3), own.at[2])
+    for off in (3, -3):
+        cross(off).wait_recv()
+    pass_on(3, 0)
+    tokens.came_across((4,))
+    expert_in((4,))
+    expert_out((4,), last)
+    cross(4).wait_recv()
+    for t in (0, 1):
+        send(t, 3, t, last[0, t] + sibin[4, t].astype(F32))
+    expert_in((2, -2))
+    expert_out((2, -2), own.at[1])
+    for off in (2, -2):
+        cross(off).wait_recv()
+    pass_on(2, 0)
+    pass_on(3, 1)
+    expert_in((1, -1))
+    expert_out((1, -1), own.at[0])
+    for off in (1, -1):
+        cross(off).wait_recv()
+    pass_on(1, 0)
+    pass_on(2, 1)
+    expert_in((0,))
+    expert_out((0,), last)
+    pass_on(1, 1)
+    cross(0).wait_recv()
+    for way in (0, 1):
+        t = 1 - way
+        hop(way, 0, t).wait_recv()
+        last[0, t] = last[0, t] + sibin[0, t].astype(F32) + ringin[way, 0, t].astype(F32)
+
+    def finish(t):
+        return last[0, t] + ringin[t, 0, t].astype(F32)
+
+    for way in (0, 1):
+        hop(way, 0, way).wait_recv()
+    finout[...] = finish(1 - c).astype(BF16)
     final = remote(finout, finin, fs.at[0], fr.at[0], sibling)
     final.start()
     here = pl.ds(pl.multiple_of(c * HALF, HALF), HALF)
     there = pl.ds(pl.multiple_of((1 - c) * HALF, HALF), HALF)
-    out[:, here] = (mixed[:, here].astype(F32) + own[c]).astype(BF16)
+    out[:, here] = (mixed[:, here].astype(F32) + finish(c)).astype(BF16)
     final.wait()
     out[:, there] = (mixed[:, there].astype(F32) + finin[...].astype(F32)).astype(BF16)
 
     for way, j, t in started:
         hop(way, j, t).wait_send()
-    for n in range(8):
-        cross(n).wait_send()
+    for off in NEAR:
+        cross(off).wait_send()
     for one in (tokens, gate_ring, up_z, up_x, down_z):
         one.sent()
     for o in range(1, NZ):
@@ -403,15 +451,10 @@
     gt = jnp.zeros((EXPERTS, T), F32)
     for i in range(TOP):
         gt = gt + jnp.where(chosen[i][None] == experts, weight[i][None], 0.0)
-    pieces = []
-    for i in range(0, HID, HD):
-        pieces += [gate_w[0][:, i : i + HD], up_w[0][:, i : i + HD]]
-    gu = jnp.concatenate(pieces, axis=1)
-    dt = jnp.pad(down_w[0].T, ((0, 0), (0, 768 - HID)))
     out = pl.pallas_call(
         kernel,
         out_shape=jax.ShapeDtypeStruct((T, D), BF16),
-        in_specs=[ANY] * 7 + [VMEM] * 3,
+        in_specs=[ANY] * 5 + [VMEM] * 6,
         out_specs=VMEM,
         scratch_shapes=[
             pltpu.VMEM((T, D), BF16),
@@ -430,15 +473,17 @@
             pltpu.VMEM((NX, 2, HD, HD), BF16),
             pltpu.VMEM((NZ, 2, HD, HD), BF16),
             pltpu.VMEM((T, D), F32),
-            pltpu.VMEM((2 * T, 768), BF16),
-            pltpu.VMEM((2, T, HALF), F32),
+            pltpu.VMEM((NY, 2, T, HD), F32),
+            pltpu.VMEM((NY, 2 * T, 768), BF16),
+            pltpu.VMEM((3, 2, 2, T, HALF), F32),
+            pltpu.VMEM((1, 2, T, HALF), F32),
             pltpu.VMEM((8, 2, T, HALF), BF16),
             pltpu.VMEM((8, 2, T, HALF), BF16),
             pltpu.VMEM((2, 4, 2, T, HALF), BF16),
             pltpu.VMEM((2, 4, 2, T, HALF), BF16),
             pltpu.VMEM((T, HALF), BF16),
             pltpu.VMEM((T, HALF), BF16),
-            DMA((7,)),
+            DMA((5,)),
             DMA((NZ,)), DMA((NZ,)), DMA((NX,)), DMA((NX,)), DMA((NZ,)), DMA((NZ,)),
             DMA((16,)), DMA((16,)), DMA((20,)), DMA((20,)),
             DMA((8,)), DMA((8,)), DMA((10,)), DMA((10,)),
@@ -450,7 +495,7 @@
             collective_id=0, has_side_effects=True, vmem_limit_bytes=56 * 2**20
         ),
         name="layer",
-    )(q[0], k[0], v[0], res[0], s0[0], gu, dt, hg[None], fg[None], gt)
+    )(q[0], k[0], v[0], res[0], s0[0], gate_w[0], up_w[0], down_w[0].T, hg[None], fg[None], gt)
     return out[None]
 
 

time: 166 us -> 154 us (0.928)
  Pallas kernels: 158 us -> 150 us
  local copies, waits for them, and re-layouts: 6.39 us -> 3.27 us
    pallas_call x1, Pallas kernels: 158 us -> 150 us  [shards(): pl.pallas_call(kernel, out_shape=jax.ShapeDtypeStruct((T, D), BF16), in_s...]
where the time goes in v3:
time: 154 us
  Pallas kernels  150 us (97%)
  local copies, waits for them, and re-layouts  3.27 us (2%)
    pallas_call x1, Pallas kernels, shards(): pl.pallas_call(kernel, out_shape=jax.ShapeDtypeStruct((T, D), BF16), in_s...  150 us
    unnamed x7, local copies, waits for them, and re-layouts  3.25 us

profile of v3, /device:TPU:1, one launch (start us, length us, event | category | flops | bytes accessed | tf_op | source)
XLA Modules:
  0.0 153.8 jit_solution(15215882638847988510)
XLA Ops:
  0.0 0.0 copy-start
  0.0 0.7 copy-done
  0.7 0.0 copy-start.1
  0.7 0.7 copy-done.1
  1.4 0.6 select_add_fusion.gt
  2.0 149.9 %layer.1 = bf16[128,2048]{1,0:T(8,128)(2,1)} custom-call(bf16[128,2048]{1,0:T(8,128)(2,1)} %bitcast.49, bf16[128,2048]{1,0:T(8,128)(2,1)} %bitcast.50, bf16[128,2048]{1,0:T(8,128)(2,1)} %bitcast.51, bf16[128,2048]{1,0:T(8,128)(2,1)} %bitcast.52, f32[16,128,128]{2,1,0:T(8,128)} %bitcast.48, bf16[64,704]{1,0:T(8,128)(2,1)} %bitcast.53, ...), custom_call_target="tpu_custom_call" | custom-call | tf_op jit(solution)/shard_map/layer/pallas_call | solution.py:454
  151.9 1.9 %copy.20 = bf16[1,128,2048]{2,1,0:T(8,128)(2,1)} copy(bf16[1,128,2048]{2,1,0:T(8,128)(2,1)} %bitcast.47) | data formatting | bytes 1048576
  (4 shorter events, 0.0 us)
Async XLA Ops:
  0.0 0.7 copy-start
  0.7 0.7 copy-start.1

commit v4 on v3

--- a/solution.py
+++ b/solution.py
@@ -161,6 +161,16 @@
     gu[x, z, :, 1280:] = jnp.concatenate([gate_in[:, 640:], up_in[:, 640:]], axis=1)
     dt[x, z] = jnp.concatenate([down_in[...], jnp.zeros((64, 768 - HID), BF16)], axis=1)
     gates[y, c] = gt[...]
+    loads[0].wait()
+    loads[1].wait()
+    for o in range(NZ):
+        for i in range(per):
+            at_cols = cols(ring(z, o, NZ) * per + i)
+            state = dot(k[:, at_cols], v[:, at_cols], TN).astype(BF16)
+            if o:
+                mine[o, i] = state
+            else:
+                parts[z, i] = state
     pl.semaphore_wait(barrier, len(near))
 
     def on_x(place):
@@ -186,19 +196,8 @@
 
     gate_ring.start(0)
 
-    loads[0].wait()
-    loads[1].wait()
-    for o in list(range(1, NZ)) + [0]:
-        owner = ring(z, o, NZ)
-        for i in range(per):
-            at_cols = cols(owner * per + i)
-            state = dot(k[:, at_cols], v[:, at_cols], TN).astype(BF16)
-            if o:
-                mine[o, i] = state
-            else:
-                parts[z, i] = state
-        if o:
-            remote(mine.at[o], parts.at[z], z1s.at[o], z1r.at[o], on_z(owner)).start()
+    for o in range(1, NZ):
+        remote(mine.at[o], parts.at[z], z1s.at[o], z1r.at[o], on_z(ring(z, o, NZ))).start()
     for w in (0, 1):
         up_z.start(w)
     up_x.start(0)
@@ -248,11 +247,6 @@
         to = ring(z, o, NZ)
         remote(back.at[to], prior.at[z], z2s.at[o], z2r.at[o], on_z(to)).start()
     prior[z] = back[z]
-    up_step(2)
-    gate_ring.step(0, 3)
-    up_x.step(0, 1)
-    for o in range(1, NX):
-        down_x(o, ring(x, -o, NX)).wait_recv()
     loads[4].wait()
 
     squares = jnp.zeros((T, 1), F32)
@@ -260,6 +254,8 @@
         owner = ring(z, -o, NZ)
         if o:
             remote(back.at[owner], prior.at[owner], z2s.at[o], z2r.at[o], on_z(owner)).wait_recv()
+        if o == 2:
+            up_step(2)
         for i in range(per):
             at_cols = cols(owner * per + i)
             attended = base[:, at_cols] + dot(q[:, at_cols], prior[owner, i])
@@ -274,14 +270,19 @@
         half = slice(w * HALF, (w + 1) * HALF)
         rows[y, c, w] = (mixed[:, half].astype(F32) * row_scale * fg[:, half]).astype(BF16)
         tokens.start(w)
-    up_step(3)
+    gate_ring.step(0, 3)
+    for o in range(1, NX):
+        down_x(o, ring(x, -o, NX)).wait_recv()
     for w in (0, 1):
         down_z.start(w)
-    gate_ring.step(0, 4)
-    up_step(4)
+    up_step(3)
+    up_x.step(0, 1)
     for n in range(1, 4):
         for w in (0, 1):
             tokens.step(w, n)
+            if n == 1 and w == 0:
+                up_step(4)
+                gate_ring.step(0, 4)
             if n == 1:
                 up_x.step(w + 1, 1)
                 down_z.step(w, 1)

time: 154 us -> 153 us (level)
  no operation moved by 1% of the time
where the time goes in v4:
time: 153 us
  Pallas kernels  149 us (97%)
  local copies, waits for them, and re-layouts  3.27 us (2%)
    pallas_call x1, Pallas kernels, shards(): pl.pallas_call(kernel, out_shape=jax.ShapeDtypeStruct((T, D), BF16), in_s...  149 us
    unnamed x7, local copies, waits for them, and re-layouts  3.25 us

profile of v4, /device:TPU:1, one launch (start us, length us, event | category | flops | bytes accessed | tf_op | source)
XLA Modules:
  0.0 152.7 jit_solution(3713700469870871280)
XLA Ops:
  0.0 0.0 copy-start
  0.0 0.7 copy-done
  0.7 0.0 copy-start.1
  0.7 0.7 copy-done.1
  1.4 0.6 select_add_fusion.gt
  2.0 148.9 %layer.1 = bf16[128,2048]{1,0:T(8,128)(2,1)} custom-call(bf16[128,2048]{1,0:T(8,128)(2,1)} %bitcast.49, bf16[128,2048]{1,0:T(8,128)(2,1)} %bitcast.50, bf16[128,2048]{1,0:T(8,128)(2,1)} %bitcast.51, bf16[128,2048]{1,0:T(8,128)(2,1)} %bitcast.52, f32[16,128,128]{2,1,0:T(8,128)} %bitcast.48, bf16[64,704]{1,0:T(8,128)(2,1)} %bitcast.53, ...), custom_call_target="tpu_custom_call" | custom-call | tf_op jit(solution)/shard_map/layer/pallas_call | solution.py:455
  150.9 1.9 %copy.20 = bf16[1,128,2048]{2,1,0:T(8,128)(2,1)} copy(bf16[1,128,2048]{2,1,0:T(8,128)(2,1)} %bitcast.47) | data formatting | bytes 1048576
  (4 shorter events, 0.0 us)
Async XLA Ops:
  0.0 0.7 copy-start
  0.7 0.7 copy-start.1
